TPU v7x, 32 devices: a whole 2x2x4 slice. The times are simulated.
32 devices in a mesh: frames: 2 (over x), date: 16 (over z, y, core).
Axes of the slice: x: 2, y: 2, z: 4, core: 2. Of those that a mesh axis runs over, the one named last changes fastest.
Arguments:
- backward_sensitivity: bfloat16 [512, 2, 256, 256], P(('frames', 'date')), parts along dimension 0, may hold values from -24 to 24
- patch_stack_samples: bfloat16 [512, 2, 256, 128], P(('frames', 'date')), parts along dimension 0, may hold values from -16 to 16
- patch_contribution_factor: float32 [512, 128], P(('frames', 'date')), parts along dimension 0, may hold values from 0.2 to 2
- neighbour_displacements: int32 [512, 128], P(('frames', 'date')), parts along dimension 0, may hold values from 0 to 255, as said below
- delay_quanta: int32 [512], P(('frames', 'date')), parts along dimension 0, may hold values from -256 to 255
- segment_correction_angles: float32 [512, 9], P(('frames', 'date')), parts along dimension 0, may hold values from -3.140625 to 3.140625
- segment_starts: int32 [16], P('frames'), parts along dimension 0, may hold values from 1 to 4095, as said below
Outputs:
- stack_grad: float32 [2, 512, 8, 4096], P(None, ('frames', 'date')), parts along dimension 1
There are 2 independent parts, one for each index of `frames`. A program takes and returns all parts, laid end to end along the dimension named above; each array names one. Nothing has to cross between parts.
Inputs may be any that keep to these rules, and one draw needn't show every extreme that they name: `neighbour_displacements`: the 128 offsets of one window are distinct. `segment_starts`: strictly increasing.
All inputs are finite; a program needn't handle non-finite values.
Results may differ from a plain program's by a relative error of at most 0.0053.
Values may be sent and summed in bfloat16 or wider, within the bound.
A program may use at most 192 MiB of HBM per device.

v0:
```python
import jax
import jax.numpy as jnp
from jax import lax
from jax.sharding import PartitionSpec as P

EPOCH_COUNT = 256
ALONG_TRACK_SIZE = 4096
RG = 8
WIN = 128
REACH = 8
QUANT = 16
SEGMENT_COUNT = 9
NBHD = 256


UPPER_LIMIT = lax.Precision.HIGHEST
epsilon = 1e-06


def shifted(block, axis, distance):
    devices = range(lax.axis_size(axis))
    route = [(i - distance, i) for i in devices if i - distance in devices]
    return lax.ppermute(block, axis, route)


def unit_angle(numerator, period):
    angle_value = 2.0 * jnp.pi / period * jnp.mod(numerator, period).astype(jnp.float32)
    return (jnp.cos(angle_value), jnp.sin(angle_value))


def complex_product(formula, left_real, left_imag, right_real, right_imag):
    out_real = jnp.einsum(formula, left_real, right_real, precision=UPPER_LIMIT) - jnp.einsum(
        formula, left_imag, right_imag, precision=UPPER_LIMIT
    )
    out_imag = jnp.einsum(formula, left_real, right_imag, precision=UPPER_LIMIT) + jnp.einsum(
        formula, left_imag, right_real, precision=UPPER_LIMIT
    )
    return (out_real, out_imag)


def window_adjoint(backward_sensitivity, patch_stack_samples, patch_contribution_factor):
    window_count = patch_stack_samples.shape[0]
    date_count = patch_stack_samples.shape[2]
    tap_total = jnp.sum(patch_contribution_factor, axis=1)
    tapered = (patch_stack_samples * patch_contribution_factor[:, None, None, :]).astype(
        jnp.bfloat16
    )
    stacked_left = tapered.reshape(window_count, 2 * date_count, WIN)
    stacked_right = patch_stack_samples.reshape(window_count, 2 * date_count, WIN)
    blocks = jnp.einsum(
        "wis,wjs->wij", stacked_left, stacked_right, preferred_element_type=jnp.float32
    )
    inverse_total = 1.0 / tap_total[:, None, None]
    cov_real = (
        blocks[:, :date_count, :date_count] + blocks[:, date_count:, date_count:]
    ) * inverse_total
    cov_imag = (
        blocks[:, date_count:, :date_count] - blocks[:, :date_count, date_count:]
    ) * inverse_total
    power_sum = jnp.diagonal(cov_real, axis1=1, axis2=2) + epsilon
    amplitude = jnp.sqrt(power_sum)
    scaling = 1.0 / (amplitude[:, :, None] * amplitude[:, None, :])
    coh_real = cov_real * scaling
    coh_imag = cov_imag * scaling
    cot_real = backward_sensitivity[:, 0].astype(jnp.float32)
    cot_imag = backward_sensitivity[:, 1].astype(jnp.float32)
    swap_real = jnp.swapaxes(cot_real, 1, 2)
    swap_imag = jnp.swapaxes(cot_imag, 1, 2)
    correction = -jnp.sum(
        (cot_real + swap_real) * coh_real + (cot_imag - swap_imag) * coh_imag, axis=2
    ) / (2.0 * power_sum)
    eye_matrix = jnp.eye(date_count, dtype=jnp.float32)
    adjusted_real = cot_real * scaling + correction[:, :, None] * eye_matrix[None, :, :]
    adjusted_imag = cot_imag * scaling
    mixed_real = (adjusted_real + jnp.swapaxes(adjusted_real, 1, 2)).astype(jnp.bfloat16)
    mixed_imag = (adjusted_imag - jnp.swapaxes(adjusted_imag, 1, 2)).astype(jnp.bfloat16)
    operator = jnp.concatenate(
        [
            jnp.concatenate([mixed_real, -mixed_imag], axis=2),
            jnp.concatenate([mixed_imag, mixed_real], axis=2),
        ],
        axis=1,
    )
    gradients = jnp.einsum(
        "wij,wjs->wis", operator, stacked_right, preferred_element_type=jnp.float32
    )
    weights = patch_contribution_factor / tap_total[:, None]
    return (
        (gradients * weights[:, None, :])
        .astype(jnp.bfloat16)
        .reshape(window_count, 2, date_count, WIN)
    )


def azimuth_line_filter(
    sample_inphase, sample_quadrature, delay_quanta, segment_correction_angles, segment_starts
):
    date_count = sample_inphase.shape[0]
    item_count = sample_inphase.shape[1]
    sample_positions = lax.iota(jnp.int32, ALONG_TRACK_SIZE)
    segment_finder = jnp.sum(
        (sample_positions[None, :] >= segment_starts[:, None]).astype(jnp.int32), axis=0
    )
    segment_chooser = (
        segment_finder[None, :] == lax.iota(jnp.int32, SEGMENT_COUNT)[:, None]
    ).astype(jnp.float32)
    along_track_rotor = jnp.dot(segment_correction_angles, segment_chooser, precision=UPPER_LIMIT)
    cosine = jnp.cos(along_track_rotor)[:, None, :]
    sine_line = jnp.sin(along_track_rotor)[:, None, :]
    input_real = cosine * sample_inphase + sine_line * sample_quadrature
    input_imag = cosine * sample_quadrature - sine_line * sample_inphase
    outer_size = 64
    inner_size = ALONG_TRACK_SIZE // outer_size
    shaped_real = input_real.reshape(date_count, item_count, outer_size, inner_size)
    shaped_imag = input_imag.reshape(date_count, item_count, outer_size, inner_size)
    outer_index = lax.iota(jnp.int32, outer_size)
    inner_index = lax.iota(jnp.int32, inner_size)
    first_cos, first_sin = unit_angle(outer_index[:, None] * outer_index[None, :], outer_size)
    second_cos, second_sin = unit_angle(inner_index[:, None] * inner_index[None, :], inner_size)
    twiddle_cos, twiddle_sin = unit_angle(
        outer_index[:, None] * inner_index[None, :], ALONG_TRACK_SIZE
    )
    section_real, section_imag = complex_product(
        "dkpq,pm->dkmq", shaped_real, shaped_imag, first_cos, -first_sin
    )
    section_real, section_imag = (
        section_real * twiddle_cos + section_imag * twiddle_sin,
        section_imag * twiddle_cos - section_real * twiddle_sin,
    )
    spec_real, spec_imag = complex_product(
        "dkmq,qn->dkmn", section_real, section_imag, second_cos, -second_sin
    )
    frequency = outer_index[:, None] + outer_size * inner_index[None, :]
    signed = jnp.where(frequency < ALONG_TRACK_SIZE // 2, frequency, frequency - ALONG_TRACK_SIZE)
    filter_cos, filter_sin = unit_angle(
        signed[None, :, :] * delay_quanta[:, None, None], ALONG_TRACK_SIZE * QUANT
    )
    filter_cos = filter_cos[:, None, :, :]
    filter_sin = filter_sin[:, None, :, :]
    spec_real, spec_imag = (
        spec_real * filter_cos - spec_imag * filter_sin,
        spec_real * filter_sin + spec_imag * filter_cos,
    )
    section_real, section_imag = complex_product(
        "dkmn,nq->dkmq", spec_real, spec_imag, second_cos, second_sin
    )
    section_real, section_imag = (
        section_real * twiddle_cos - section_imag * twiddle_sin,
        section_real * twiddle_sin + section_imag * twiddle_cos,
    )
    out_real, out_imag = complex_product(
        "dkmq,mp->dkpq", section_real, section_imag, first_cos, first_sin
    )
    restored = jnp.stack(
        [
            out_real.reshape(date_count, item_count, ALONG_TRACK_SIZE),
            out_imag.reshape(date_count, item_count, ALONG_TRACK_SIZE),
        ]
    )
    return restored * (1.0 / ALONG_TRACK_SIZE)


def on_device(
    backward_sensitivity,
    patch_stack_samples,
    patch_contribution_factor,
    neighbour_displacements,
    delay_quanta,
    segment_correction_angles,
    segment_starts,
):
    window_count = patch_stack_samples.shape[0]
    slot_grads = window_adjoint(
        backward_sensitivity, patch_stack_samples, patch_contribution_factor
    )
    tile_lines = WIN // RG
    hood_lines = NBHD // RG
    own_lines = window_count * tile_lines
    seat_labels = lax.iota(jnp.int32, NBHD)
    segment_chooser = (neighbour_displacements[:, :, None] == seat_labels[None, None, :]).astype(
        jnp.bfloat16
    )
    spread = jnp.einsum(
        "wcs,wsn->wcn",
        slot_grads.reshape(window_count, 2 * EPOCH_COUNT, WIN),
        segment_chooser,
        preferred_element_type=jnp.float32,
    )
    block_count = hood_lines // tile_lines
    pieces = spread.reshape(window_count, 2 * EPOCH_COUNT, RG, block_count, tile_lines)
    extended = jnp.zeros(
        (window_count + block_count - 1, 2 * EPOCH_COUNT, RG, tile_lines), jnp.float32
    )
    for block_index in range(block_count):
        extended = extended.at[block_index : block_index + window_count].add(
            pieces[:, :, :, block_index, :]
        )
    extended = jnp.transpose(extended, (1, 2, 0, 3)).reshape(
        2 * EPOCH_COUNT, RG, (window_count + block_count - 1) * tile_lines
    )
    lower_rim = extended[:, :, :REACH]
    upper_rim = extended[:, :, REACH + own_lines :]
    middle = extended[:, :, REACH : REACH + own_lines]
    from_next = shifted(lower_rim.astype(jnp.bfloat16), "date", -1).astype(lower_rim.dtype)
    from_prev = shifted(upper_rim.astype(jnp.bfloat16), "date", 1).astype(upper_rim.dtype)
    zeros_pad = own_lines - REACH
    pixels = (
        middle
        + jnp.pad(from_next, ((0, 0), (0, 0), (zeros_pad, 0)))
        + jnp.pad(from_prev, ((0, 0), (0, 0), (0, zeros_pad)))
    )
    pixels = pixels.reshape(2, EPOCH_COUNT, RG, own_lines)
    sample_raster = lax.all_to_all(pixels, "date", split_axis=1, concat_axis=3, tiled=True)
    return azimuth_line_filter(
        sample_raster[0], sample_raster[1], delay_quanta, segment_correction_angles, segment_starts
    )


def solution(mesh):
    return jax.shard_map(
        on_device,
        mesh=mesh,
        in_specs=(
            P(("frames", "date"), None, None, None),
            P(("frames", "date"), None, None, None),
            P(("frames", "date"), None),
            P(("frames", "date"), None),
            P(("frames", "date")),
            P(("frames", "date"), None),
            P("frames"),
        ),
        out_specs=P(None, ("frames", "date"), None, None),
        check_vma=False,
    )
```

profile of v0, /device:TPU:15, one launch (start us, length us, event | category | flops | bytes accessed | tf_op | source)
XLA Modules:
  0.0 369.8 jit_solution(9881099199280457646)
XLA Ops:
  6.3 5.7 %copy-done.2 = f32[16,512,512]{1,2,0:T(8,128)} copy-done((f32[16,512,512]{1,2,0:T(8,128)}, f32[16,512,512]{1,2,0:T(8,128)S(1)}, u32[]{:S(2)}) %copy-start.2) | copy-done | bytes 16777240
  14.6 17.9 %copy.155 = f32[16,256,256]{0,2,1:T(8,128)} copy(f32[16,256,256]{1,2,0:T(8,128)} %fusion.14) | data formatting | bytes 8388608 | tf_op jit(solution)/shard_map/mul | solution.py:54
  35.0 5.5 %bitcast_convert_fusion = (f32[16,256,256]{2,1,0:T(8,128)}, bf16[16,1,256,256]{3,2,1,0:T(8,128)(2,1)}) fusion(bf16[16,2,256,256]{3,2,1,0:T(8,128)(2,1)} %param.11), kind=kLoop, calls=%fused_computation.59 | loop fusion | flops 1048576 | bytes 10485760 | tf_op jit(solution)/shard_map/convert_element_type | solution.py:65
  45.7 5.4 %copy.161 = f32[16,256,256]{2,1,0:T(8,128)} copy(f32[16,256,256]{1,2,0:T(8,128)} %bitcast_convert_fusion.1) | data formatting | bytes 8388608 | tf_op jit(solution)/shard_map/convert_element_type | solution.py:66
  51.1 5.4 %copy.158 = f32[16,256,256]{1,2,0:T(8,128)} copy(f32[16,256,256]{2,1,0:T(8,128)} %get-tuple-element.35) | data formatting | bytes 8388608 | tf_op jit(solution)/shard_map/convert_element_type | solution.py:65
  56.5 5.4 %bitcast_add_fusion.1 = f32[16,256,256]{2,1,0:T(8,128)} fusion(f32[16,256,256]{1,2,0:T(8,128)} %copy.158, bf16[16,2,256,256]{3,2,1,0:T(8,128)(2,1)} %param.11), kind=kLoop, calls=%fused_computation.37 | loop fusion | flops 2097152 | bytes 10485760 | tf_op jit(solution)/shard_map/add | solution.py:70
  61.8 5.4 %copy.159 = f32[16,256,256]{1,2,0:T(8,128)} copy(f32[16,256,256]{2,1,0:T(8,128)} %bitcast_add_fusion.1) | data formatting | bytes 8388608 | tf_op jit(solution)/shard_map/add | solution.py:70
  67.2 13.2 %convert_multiply_fusion = (f32[16,256,256]{1,2,0:T(8,128)}, f32[16,256]{1,0:T(8,128)S(1)}, f32[16,256,256]{1,2,0:T(8,128)}) fusion(bf16[16,1,256,256]{2,3,0,1:T(8,128)(2,1)S(1)} %copy.204, f32[16,256]{1,0:T(8,128)S(1)} %sqrt_bitcast_fusion, f32[16]{0:T(128)S(1)} %broadcast_divide_fusion.1, f32[16,512,512]{1,2,0:T(8,128)} %copy-done.2, ...), kind=kLoop, calls=%fused_computation.60 | loop fusion | flops 15724544 | bytes 35701248 | tf_op jit(solution)/shard_map/mul | solution.py:74
  80.4 5.4 %copy.157 = f32[16,256,256]{2,1,0:T(8,128)} copy(f32[16,256,256]{1,2,0:T(8,128)} %get-tuple-element.45) | data formatting | bytes 8388608 | tf_op jit(solution)/shard_map/div | solution.py:62
  85.8 4.5 %multiply_add_fusion.4 = f32[16,256,256]{2,1,0:T(8,128)} fusion(f32[16,256,256]{2,1,0:T(8,128)} %copy.157, f32[256,256]{1,0:T(8,128)S(1)} %fusion.52, f32[16,256]{1,0:T(8,128)S(1)} %bitcast_divide_fusion, bf16[16,2,256,256]{3,2,1,0:T(8,128)(2,1)} %param.11), kind=kLoop, calls=%fused_computation.49 | loop fusion | flops 4194304 | bytes 10764288 | tf_op jit(solution)/shard_map/add | solution.py:73
  90.3 5.4 %copy.162 = f32[16,256,256]{1,2,0:T(8,128)} copy(f32[16,256,256]{2,1,0:T(8,128)} %multiply_add_fusion.4) | data formatting | bytes 8388608 | tf_op jit(solution)/shard_map/add | solution.py:73
  95.7 5.4 %fusion.26 = bf16[16,256,256]{1,2,0:T(8,128)(2,1)} fusion(f32[16,256,256]{1,2,0:T(8,128)} %copy.162, f32[16,256,256]{2,1,0:T(8,128)} %multiply_add_fusion.4), kind=kLoop, calls=%fused_computation.35 | loop fusion | flops 2097152 | bytes 10485760 | tf_op jit(solution)/shard_map/convert_element_type | solution.py:75
  101.1 5.4 %copy.163 = f32[16,256,256]{2,1,0:T(8,128)} copy(f32[16,256,256]{1,2,0:T(8,128)} %get-tuple-element.39) | data formatting | bytes 8388608 | tf_op jit(solution)/shard_map/mul | solution.py:74
  110.7 18.9 %fusion.33 = f32[16,512,256]{1,2,0:T(8,128)} fusion(bf16[16,512,128]{2,1,0:T(8,128)(2,1)} %bitcast.145, bf16[16,256,256]{1,2,0:T(8,128)(2,1)} %fusion.26, bf16[16,256,256]{1,2,0:T(8,128)(2,1)} %get-tuple-element.30, bf16[16,256,256]{1,2,0:T(8,128)(2,1)} %get-tuple-element.29, f32[16,128]{1,0:T(8,128)S(1)} %broadcast_divide_fusion, s32[16,128]{1,0:T(8,128)S(1)} %copy-done.10), kind=kOutput, calls=%fused_computation.58 | convolution fusion | flops 1646788608 | bytes 16793600 | tf_op jit(solution)/shard_map/wcs,wsn->wcn/dot_general | solution.py:183
  129.7 4.6 %fusion.173 = (f32[16,512,8,1,16]{1,4,3,2,0:T(8,128)S(1)}, f32[16,512,8,1,16]{1,4,3,2,0:T(8,128)S(1)}) fusion(f32[16,512,8,2,16]{1,4,3,2,0:T(8,128)} %bitcast.148), kind=kLoop, calls=%fused_computation.205 | loop fusion | bytes 16777216 | tf_op jit(solution)/shard_map/slice | solution.py:196
  147.3 5.9 %reshape.228 = f32[2,256,8,256]{1,0,3,2:T(2,128)} reshape(f32[512,8,256]{0,2,1:T(8,128)} %fusion.8) | data formatting | bytes 8388608 | tf_op jit(solution)/shard_map/reshape | solution.py:212
  153.2 5.5 %copy.167 = f32[2,256,8,256]{3,2,0,1:T(8,128)} copy(f32[2,256,8,256]{1,0,3,2:T(2,128)} %reshape.228) | data formatting | bytes 8388608 | tf_op jit(solution)/shard_map/reshape | solution.py:212
  158.7 7.2 %all-to-all-start = ((f32[2,256,8,256]{3,2,0,1:T(8,128)}), f32[2,256,8,256]{3,2,0,1:T(8,128)}, u32[]{:S(2)}, u32[]{:S(2)}) async-start(f32[2,256,8,256]{3,2,0,1:T(8,128)} %copy.167), calls=%async_computation | async-start | bytes 8388608 | tf_op jit(solution)/shard_map/all_to_all | solution.py:213
  170.7 87.6 %all-to-all-done = f32[2,256,8,256]{3,2,0,1:T(8,128)} async-done(((f32[2,256,8,256]{3,2,0,1:T(8,128)}), f32[2,256,8,256]{3,2,0,1:T(8,128)}, u32[]{:S(2)}, u32[]{:S(2)}) %all-to-all-start) | async-done | bytes 4194336 | tf_op jit(solution)/shard_map/all_to_all | solution.py:213
  278.0 7.7 %fusion.42 = f32[64,16,8,64]{3,0,2,1:T(8,128)S(1)} fusion(f32[16,8,64,64]{3,2,1,0:T(8,128)} %squeeze.5, f32[16,8,64,64]{3,2,1,0:T(8,128)} %squeeze.4, f32[16,64,64]{2,1,0:T(8,128)S(1)} %mul.529, f32[16,64,64]{2,1,0:T(8,128)S(1)} %mul.505), kind=kOutput, calls=%fused_computation.70 | convolution fusion | flops 404287488 | bytes 6815744 | tf_op jit(solution)/shard_map/dkpq,pm->dkmq/dot_general | solution.py:35
  335.4 5.6 %fusion.39 = f32[64,16,8,64]{3,0,2,1:T(8,128)} fusion(f32[16,8,64,64]{3,2,1,0:T(8,128)S(1)} %convolution_add_fusion, f32[16,8,64,64]{3,2,1,0:T(8,128)S(1)} %convolution_subtract_fusion, f32[64,64]{1,0:T(8,128)S(1)} %copy.172, f32[64,64]{1,0:T(8,128)S(1)} %copy.171), kind=kOutput, calls=%fused_computation.64 | convolution fusion | flops 404283392 | bytes 6324224 | tf_op jit(solution)/shard_map/dkmq,mp->dkpq/dot_general | solution.py:35
  341.0 5.5 %subtract_bitcast_fusion = f32[16,8,64,64]{3,2,1,0:T(8,128)} fusion(f32[64,16,8,64]{3,0,2,1:T(8,128)S(1)} %fusion.40, f32[16,8,64,64]{3,2,1,0:T(8,128)S(1)} %convolution_add_fusion, f32[16,8,64,64]{3,2,1,0:T(8,128)S(1)} %convolution_subtract_fusion, f32[64,64]{1,0:T(8,128)S(1)} %copy.172, f32[64,64]{1,0:T(8,128)S(1)} %copy.171), kind=kOutput, calls=%fused_computation.39 | convolution fusion | flops 404807680 | bytes 8421376 | tf_op jit(solution)/shard_map/dkmq,mp->dkpq/dot_general | solution.py:32
  350.0 10.6 %add_bitcast_fusion = f32[16,8,64,64]{3,2,1,0:T(8,128)} fusion(f32[64,16,8,64]{3,0,2,1:T(8,128)} %fusion.39, f32[16,8,64,64]{3,2,1,0:T(8,128)} %copy-done.4, f32[16,8,64,64]{3,2,1,0:T(8,128)} %copy-done.3, f32[64,64]{1,0:T(8,128)S(1)} %copy.172, f32[64,64]{1,0:T(8,128)S(1)} %copy.171), kind=kOutput, calls=%fused_computation.38 | convolution fusion | flops 404807680 | bytes 8421376 | tf_op jit(solution)/shard_map/dkmq,mp->dkpq/dot_general | solution.py:35
  360.6 4.8 %stack_reshape.7 = f32[1,16,8,4096]{3,2,1,0:T(8,128)} reshape(f32[16,8,64,64]{3,2,1,0:T(8,128)} %add_bitcast_fusion) | data formatting | bytes 4194304 | tf_op jit(solution)/shard_map/stack;reshape | solution.py:154
  (77 shorter events, 115.6 us)
Async XLA Ops:
  0.0 166.0 %copy-start = (f32[16,9]{1,0:T(8,128)S(1)}, f32[16,9]{1,0:T(8,128)}, u32[]{:S(2)}) copy-start(f32[16,9]{1,0:T(8,128)} %param.16) | copy-start | bytes 1732
  0.0 4.0 %copy-start.7 = (bf16[16,2,256,128]{3,2,1,0:T(8,128)(2,1)S(1)}, bf16[16,2,256,128]{3,2,1,0:T(8,128)(2,1)}, u32[]{:S(2)}) copy-start(bf16[16,2,256,128]{3,2,1,0:T(8,128)(2,1)} %param.12) | copy-start | bytes 6291460
  6.3 5.7 %copy-start.2 = (f32[16,512,512]{1,2,0:T(8,128)}, f32[16,512,512]{1,2,0:T(8,128)S(1)}, u32[]{:S(2)}) copy-start(f32[16,512,512]{1,2,0:T(8,128)S(1)} %fusion.176) | copy-start | bytes 50331652
  106.5 4.3 %copy-start.10 = (s32[16,128]{1,0:T(8,128)S(1)}, s32[16,128]{1,0:T(8,128)}, u32[]{:S(2)}) copy-start(s32[16,128]{1,0:T(8,128)} %param.14) | copy-start | bytes 24580
  137.0 6.5 %collective-permute-start = (bf16[512,8,8]{0,2,1:T(8,128)(2,1)S(1)}, bf16[512,8,8]{0,2,1:T(8,128)(2,1)S(1)}, u32[]{:S(2)}, u32[]{:S(2)}) collective-permute-start(bf16[512,8,8]{0,2,1:T(8,128)(2,1)S(1)} %get-tuple-element.37), channel_id=1, source_target_pairs={{1,0},{2,1},{3,2},{4,3},{5,4},{6,5},{7,6},{8,7},{9,8},{10,9},{11,1... | collective-permute-start | bytes 196616 | tf_op jit(solution)/shard_map/ppermute | solution.py:23
  139.6 5.2 %collective-permute-start.1 = (bf16[512,8,8]{0,2,1:T(8,128)(2,1)S(1)}, bf16[512,8,8]{0,2,1:T(8,128)(2,1)S(1)}, u32[]{:S(2)}, u32[]{:S(2)}) collective-permute-start(bf16[512,8,8]{0,2,1:T(8,128)(2,1)S(1)} %get-tuple-element.38), channel_id=1, source_target_pairs={{0,1},{1,2},{2,3},{3,4},{4,5},{5,6},{6,7},{7,8},{8,9},{9,10},{10,1... | collective-permute-start | bytes 196616 | tf_op jit(solution)/shard_map/ppermute | solution.py:23
  158.7 7.2 %copy-start.9 = (s32[8]{0:T(128)S(1)}, s32[8]{0:T(128)}, u32[]{:S(2)}) copy-start(s32[8]{0:T(128)} %param.17) | copy-start | bytes 100
  158.7 9.9 %copy-start.8 = (s32[16]{0:T(128)S(1)}, s32[16]{0:T(128)}, u32[]{:S(2)}) copy-start(s32[16]{0:T(128)} %param.15) | copy-start | bytes 196
  158.7 99.7 %all-to-all-start = ((f32[2,256,8,256]{3,2,0,1:T(8,128)}), f32[2,256,8,256]{3,2,0,1:T(8,128)}, u32[]{:S(2)}, u32[]{:S(2)}) async-start(f32[2,256,8,256]{3,2,0,1:T(8,128)} %copy.167), calls=%async_computation | async-start | bytes 8388608 | tf_op jit(solution)/shard_map/all_to_all | solution.py:213
  278.0 7.7 %copy-start.5 = (f32[16,8,64,64]{3,2,1,0:T(8,128)S(1)}, f32[16,8,64,64]{3,2,1,0:T(8,128)}, u32[]{:S(2)}) copy-start(f32[16,8,64,64]{3,2,1,0:T(8,128)} %squeeze.4) | copy-start | bytes 6291460
  278.0 7.7 %copy-start.6 = (f32[16,8,64,64]{3,2,1,0:T(8,128)S(1)}, f32[16,8,64,64]{3,2,1,0:T(8,128)}, u32[]{:S(2)}) copy-start(f32[16,8,64,64]{3,2,1,0:T(8,128)} %squeeze.5) | copy-start | bytes 6291460
  327.1 13.9 %copy-start.3 = (f32[16,8,64,64]{3,2,1,0:T(8,128)}, f32[16,8,64,64]{3,2,1,0:T(8,128)S(1)}, u32[]{:S(2)}) copy-start(f32[16,8,64,64]{3,2,1,0:T(8,128)S(1)} %convolution_subtract_fusion) | copy-start | bytes 6291460
  331.2 9.8 %copy-start.4 = (f32[16,8,64,64]{3,2,1,0:T(8,128)}, f32[16,8,64,64]{3,2,1,0:T(8,128)S(1)}, u32[]{:S(2)}) copy-start(f32[16,8,64,64]{3,2,1,0:T(8,128)S(1)} %convolution_add_fusion) | copy-start | bytes 6291460
  360.6 9.0 %copy-start.1 = (f32[16,9]{1,0:T(8,128)S(1)}, f32[16,9]{1,0:T(8,128)}, u32[]{:S(2)}) copy-start(f32[16,9]{1,0:T(8,128)} %param.16) | copy-start | bytes 1732
where the time goes:
time: 369 us; the launch traced here: 370 us
  local copies, waits for them, and re-layouts  107 us (29%)
  matrix products  102 us (28%)
  waiting for transfers between devices  88.9 us (24%)
  other arithmetic  57.9 us (16%)
  starting transfers between devices  13.7 us (4%)
    all_to_all x1, waiting for transfers between devices, on_device(): lax.all_to_all(pixels, 'date', split_axis=1, concat_axis=3, tiled=True)  87.6 us
    dot_general x4, matrix products, complex_product(): jnp.einsum(formula, left_imag, right_real, precision=UPPER_LIMIT)  22.9 us
    dot_general x4, matrix products, complex_product(): jnp.einsum(formula, left_real, right_imag, precision=UPPER_LIMIT)  21.6 us
    dot_general x1, matrix products, on_device(): jnp.einsum('wcs,wsn->wcn', slot_grads.reshape(window_count, 2 * EPOCH_COU...  18.9 us
    dot_general x4, matrix products, complex_product(): jnp.einsum(formula, left_imag, right_imag, precision=UPPER_LIMIT)  18.3 us
    mul x1, local copies, waits for them, and re-layouts, window_adjoint(): (blocks[:, :date_count, :date_count] + blocks[:, date_count:, date_count:...  17.9 us
    dot_general x4, matrix products, complex_product(): jnp.einsum(formula, left_real, right_real, precision=UPPER_LIMIT)  16.2 us
    mul x1, other arithmetic, window_adjoint(): adjusted_imag = cot_imag * scaling  13.2 us
  transfers between devices with their start and end apart: 3, of which 2 were waited for; matrix products, arithmetic and copies ran while one was open for 1% of the time, Pallas kernels for 0%

commit v1 on v0

v1 whole, which is shorter than its diff:
```python
import functools

import jax
import jax.numpy as jnp
import numpy as np
from jax import lax
from jax.experimental import pallas as pl
from jax.experimental.pallas import tpu as pltpu
from jax.sharding import PartitionSpec as P

EPOCHS = 256
LINES = 4096
RG = 8
WIN = 128
QUANT = 16
SEGMENTS = 9
MESH = pl.DeviceIdType.MESH
F32 = jnp.float32
BF16 = jnp.bfloat16


def windows_kernel(
    n, dates, wpd,
    g_hbm, z_hbm, wt_ref, disp_ref, x_hbm,
    gbuf, zbuf, lo_last, hi, pix, halo_out, halo_in, sendbuf,
    in_sem, halo_sem, send_sem, recv_sem, local_sem,
):
    me = lax.axis_index("date")
    chunks = wpd // 8

    def input_copies(w):
        return (
            pltpu.make_async_copy(g_hbm.at[w], gbuf.at[w], in_sem.at[w, 0]),
            pltpu.make_async_copy(z_hbm.at[w], zbuf.at[w], in_sem.at[w, 1]),
        )

    for w in [wpd - 1] + list(range(wpd - 1)):
        for copy in input_copies(w):
            copy.start()

    barrier = pltpu.get_barrier_semaphore()
    for k in range(1, n):
        pl.semaphore_signal(
            barrier, inc=1, device_id={"date": lax.rem(me + k, n)}, device_id_type=MESH
        )
    pl.semaphore_wait(barrier, n - 1)

    def window(w):
        for copy in input_copies(w):
            copy.wait()
        z0, z1 = zbuf[w, 0], zbuf[w, 1]
        z0f, z1f = z0.astype(F32), z1.astype(F32)
        wt = wt_ref[pl.ds(w, 1), :]
        inverse = 1.0 / jnp.sum(wt, axis=1, keepdims=True)
        q0 = (z0f * wt).astype(BF16).astype(F32)
        q1 = (z1f * wt).astype(BF16).astype(F32)
        power = jnp.sum(q0 * z0f + q1 * z1f, axis=1, keepdims=True) * inverse + 1e-6
        amp = lax.rsqrt(power)
        eye = lax.broadcasted_iota(jnp.int32, (EPOCHS, EPOCHS), 0) == lax.broadcasted_iota(
            jnp.int32, (EPOCHS, EPOCHS), 1
        )
        amp_row = jnp.sum(jnp.where(eye, amp, 0.0), axis=0, keepdims=True)
        scale = amp * amp_row
        g0, g1 = gbuf[w, 0], gbuf[w, 1]
        m0 = ((g0.astype(F32) + g0.T.astype(F32)) * scale).astype(BF16)
        m1 = ((g1.astype(F32) - g1.T.astype(F32)) * scale).astype(BF16)
        zcat = jnp.concatenate([z0, z1], axis=1)
        a0 = jnp.dot(m0, zcat, preferred_element_type=F32)
        a1 = jnp.dot(m1, zcat, preferred_element_type=F32)
        gre = a0[:, :WIN] - a1[:, WIN:]
        gim = a1[:, :WIN] + a0[:, WIN:]
        twice = -(jnp.sum(q0 * gre + q1 * gim, axis=1, keepdims=True) * inverse) / power
        share = wt * inverse
        s0 = ((gre + twice * z0f) * share).astype(BF16)
        s1 = ((gim + twice * z1f) * share).astype(BF16)
        seat = lax.broadcasted_iota(jnp.int32, (2 * WIN, WIN), 0)
        near = (seat >= WIN).astype(jnp.int32)
        inner = seat - near * WIN
        line = inner % 16 + 16 * near
        label = (inner // 16) * 32 + line
        first = jnp.logical_and(me == 0, w == 0).astype(jnp.int32)
        final = jnp.logical_and(me == n - 1, w == wpd - 1).astype(jnp.int32)
        off = (line < 8).astype(jnp.int32) * first + (line >= 24).astype(jnp.int32) * final
        label = label - off * 4096
        chooser = (label == disp_ref[pl.ds(w, 1), :]).astype(F32).astype(BF16)
        dims = (((1,), (1,)), ((), ()))
        return (
            lax.dot_general(s0, chooser, dims, preferred_element_type=F32),
            lax.dot_general(s1, chooser, dims, preferred_element_type=F32),
        )

    spread = window(wpd - 1)
    for c in range(2):
        lo_last[pl.ds(c * EPOCHS, EPOCHS), :] = spread[c][:, :WIN]
        halo_out[pl.ds(c * EPOCHS, EPOCHS), :] = spread[c][:, WIN:].astype(BF16)
    halo = pltpu.make_async_remote_copy(
        src_ref=halo_out, dst_ref=halo_in, send_sem=halo_sem.at[0], recv_sem=halo_sem.at[1],
        device_id={"date": lax.rem(me + 1, n)}, device_id_type=MESH,
    )
    halo.start()
    hi[...] = jnp.zeros_like(hi)

    lane = lax.broadcasted_iota(jnp.int32, (2 * dates, WIN), 1)

    def send_copy(g, k):
        e = lax.rem(me + k, n)
        return pltpu.make_async_remote_copy(
            src_ref=sendbuf.at[g, e], dst_ref=x_hbm.at[g, me],
            send_sem=send_sem.at[g, k], recv_sem=recv_sem.at[g, k],
            device_id={"date": e}, device_id_type=MESH,
        )

    for g in range(chunks):
        count = 8 if g < chunks - 1 else 7

        def step(b, carry):
            spread = window(b + 8 * g)
            for c in range(2):
                rows = pl.ds(c * EPOCHS, EPOCHS)
                pix[b, rows, :] = spread[c][:, :WIN] + hi[rows, :]
                hi[rows, :] = spread[c][:, WIN:]
            return carry

        lax.fori_loop(0, count, step, 0)
        if g == 0:
            halo.wait()
            pix[0] = pix[0] + halo_in[...].astype(F32)
        if g == chunks - 1:
            pix[7] = lo_last[...] + hi[...]

        def relayout(e):
            items = []
            for b in range(8):
                items.append(jnp.concatenate([
                    pix[b, pl.ds(pl.multiple_of(e * dates, 8), dates), :],
                    pix[b, pl.ds(pl.multiple_of(EPOCHS + e * dates, 8), dates), :],
                ], axis=0))
            for bit in (4, 2, 1):
                keep = (lane // (16 * bit)) % 2 == 0
                for b in range(8):
                    if b & bit == 0:
                        low, high = items[b], items[b + bit]
                        items[b] = jnp.where(keep, low, pltpu.roll(high, 16 * bit, 1))
                        items[b + bit] = jnp.where(keep, pltpu.roll(low, WIN - 16 * bit, 1), high)
            for column in range(8):
                sendbuf[g, e, column] = items[column].astype(BF16)

        def send(k, carry):
            relayout(lax.rem(me + k, n))
            send_copy(g, k).start()
            return carry

        lax.fori_loop(1, n, send, 0)
        relayout(me)
        pltpu.make_async_copy(sendbuf.at[g, me], x_hbm.at[g, me], local_sem.at[g]).start()

    for g in range(chunks):
        pltpu.make_async_copy(sendbuf.at[g, me], x_hbm.at[g, me], local_sem.at[g]).wait()

        def drain(k, carry):
            send_copy(g, k).wait()
            return carry

        lax.fori_loop(1, n, drain, 0)


def windows_call(n, g, z, wt, disp):
    wpd = g.shape[0]
    dates = EPOCHS // n
    chunks = wpd // 8
    return pl.pallas_call(
        functools.partial(windows_kernel, n, dates, wpd),
        out_shape=jax.ShapeDtypeStruct((chunks, n, RG, 2 * dates, WIN), BF16),
        in_specs=[pl.BlockSpec(memory_space=pl.ANY)] * 2
        + [pl.BlockSpec(memory_space=pltpu.VMEM)] * 2,
        out_specs=pl.BlockSpec(memory_space=pl.ANY),
        scratch_shapes=[
            pltpu.VMEM((wpd, 2, EPOCHS, EPOCHS), BF16),
            pltpu.VMEM((wpd, 2, EPOCHS, WIN), BF16),
            pltpu.VMEM((2 * EPOCHS, WIN), F32),
            pltpu.VMEM((2 * EPOCHS, WIN), F32),
            pltpu.VMEM((8, 2 * EPOCHS, WIN), F32),
            pltpu.VMEM((2 * EPOCHS, WIN), BF16),
            pltpu.VMEM((2 * EPOCHS, WIN), BF16),
            pltpu.VMEM((chunks, n, RG, 2 * dates, WIN), BF16),
            pltpu.SemaphoreType.DMA((wpd, 2)),
            pltpu.SemaphoreType.DMA((2,)),
            pltpu.SemaphoreType.DMA((chunks, n)),
            pltpu.SemaphoreType.DMA((chunks, n)),
            pltpu.SemaphoreType.DMA((chunks,)),
        ],
        compiler_params=pltpu.CompilerParams(
            collective_id=0, has_side_effects=True, vmem_limit_bytes=40 * 1024 * 1024
        ),
        name="windows",
    )(g, z, wt, disp)


def butterfly(real, imag, sign):
    n = len(real)
    if n == 1:
        return real, imag
    er, ei = butterfly(real[0::2], imag[0::2], sign)
    our, oui = butterfly(real[1::2], imag[1::2], sign)
    half = n // 2
    out_r, out_i = [None] * n, [None] * n
    for k in range(half):
        xr, xi = our[k], oui[k]
        if k == 0:
            tr, ti = xr, xi
        elif 4 * k == n:
            tr, ti = (xi, -xr) if sign < 0 else (-xi, xr)
        else:
            angle = sign * 2.0 * np.pi * k / n
            c, s = float(np.cos(angle)), float(np.sin(angle))
            tr, ti = xr * c - xi * s, xr * s + xi * c
        out_r[k], out_i[k] = er[k] + tr, ei[k] + ti
        out_r[k + half], out_i[k + half] = er[k] - tr, ei[k] - ti
    return out_r, out_i


def split(value):
    high = value.astype(BF16)
    return high, (value - high.astype(F32)).astype(BF16)


def filter_kernel(
    n, dates, reach,
    starts_ref, x_ref, delay_ref, angle_ref, mats_ref, tw_ref, o_hbm,
    phase, twist, xp, yh, yl, u, out, out_sem,
):
    chunks = reach // WIN
    unit = float(2.0 * np.pi / (LINES * QUANT))
    period = LINES * QUANT
    delay = delay_ref[...] + 8 * QUANT
    cosines, sines = jnp.cos(angle_ref[...]), jnp.sin(angle_ref[...])
    for s in range(n):
        position = s * reach + lax.broadcasted_iota(jnp.int32, (dates, reach), 1) - 8
        position = jnp.where(position < 0, position + LINES, position)
        pc = jnp.broadcast_to(cosines[:, 0:1], (dates, reach))
        ps = jnp.broadcast_to(sines[:, 0:1], (dates, reach))
        for j in range(1, SEGMENTS):
            later = position >= starts_ref[j - 1]
            pc = jnp.where(later, cosines[:, j : j + 1], pc)
            ps = jnp.where(later, sines[:, j : j + 1], ps)
        phase[0, s], phase[1, s] = pc, ps
    rows = (lax.broadcasted_iota(jnp.int32, (dates, WIN), 1) * delay) & (period - 1)
    row_angle = rows.astype(F32) * unit
    row_c, row_s = jnp.cos(row_angle), jnp.sin(row_angle)
    for k in range(n):
        bc, bs = tw_ref[0, k : k + 1, :], tw_ref[1, k : k + 1, :]
        rc, rs = row_c[:, k : k + 1], row_s[:, k : k + 1]
        twist[0, k] = rc * bc + rs * bs
        twist[1, k] = rs * bc - rc * bs
    lanes = lax.broadcasted_iota(jnp.int32, (dates, reach), 1)
    lanes = jnp.where(lanes < reach // 2, lanes, lanes - reach) * n
    lane_angle = ((lanes * delay) & (period - 1)).astype(F32) * unit
    lane_c = jnp.concatenate([jnp.cos(lane_angle)] * n, axis=0)
    lane_s = jnp.concatenate([jnp.sin(lane_angle)] * n, axis=0)

    def product(which):
        high, low = yh[...], yl[...]
        mh, ml = mats_ref[which, 0], mats_ref[which, 1]
        return (
            jnp.dot(high, mh, preferred_element_type=F32)
            + jnp.dot(low, mh, preferred_element_type=F32)
            + jnp.dot(high, ml, preferred_element_type=F32)
        )

    def column(col, carry):
        for lt in range(chunks):
            lane = pl.ds(lt * WIN, WIN)
            for s in range(n):
                x = x_ref[lt, s, col].astype(F32)
                xr, xi = x[:dates], x[dates:]
                pc, ps = phase[0, s, :, lane], phase[1, s, :, lane]
                xp[0, s] = pc * xr + ps * xi
                xp[1, s] = pc * xi - ps * xr
            for dh in range(dates // 8):
                row = pl.ds(dh * 8, 8)
                yr, yi = butterfly(
                    [xp[0, s, row, :] for s in range(n)], [xp[1, s, row, :] for s in range(n)], -1
                )
                for k in range(n):
                    tc, ts = twist[0, k, row, lane], twist[1, k, row, lane]
                    u[pl.ds(k * dates + dh * 8, 8), lane] = yr[k] * tc - yi[k] * ts
                    u[pl.ds(k * dates + dh * 8, 8), pl.ds(reach + lt * WIN, WIN)] = (
                        yr[k] * ts + yi[k] * tc
                    )
        yh[...], yl[...] = split(u[...])
        spec = product(0)
        sr, si = spec[:, :reach], spec[:, reach:]
        rh, rl = split(sr * lane_c - si * lane_s)
        ih, il = split(sr * lane_s + si * lane_c)
        yh[:, :reach], yh[:, reach:] = rh, ih
        yl[:, :reach], yl[:, reach:] = rl, il
        u[...] = product(1)
        for lt in range(chunks):
            lane = pl.ds(lt * WIN, WIN)
            for dh in range(dates // 8):
                vr, vi = [], []
                for k in range(n):
                    ur = u[pl.ds(k * dates + dh * 8, 8), lane]
                    ui = u[pl.ds(k * dates + dh * 8, 8), pl.ds(reach + lt * WIN, WIN)]
                    bc, bs = tw_ref[0, k : k + 1, lane], tw_ref[1, k : k + 1, lane]
                    vr.append(ur * bc - ui * bs)
                    vi.append(ur * bs + ui * bc)
                vr, vi = butterfly(vr, vi, 1)
                for h in range(n):
                    for c, v in ((0, vr[h]), (1, vi[h])):
                        out[h * chunks + lt, pl.ds((c * dates + dh * 8) * RG + col, 8, stride=RG), :] = v
        return carry

    lax.fori_loop(0, RG, column, 0)
    copies = [
        pltpu.make_async_copy(out.at[t], o_hbm.at[:, pl.ds(t * WIN, WIN)], out_sem.at[t])
        for t in range(LINES // WIN)
    ]
    for copy in copies:
        copy.start()
    for copy in copies:
        copy.wait()


def filter_call(n, x, delay, angles, starts):
    dates = delay.shape[0]
    reach = LINES // n
    grid = np.outer(np.arange(reach), np.arange(reach)) % reach * (2.0 * np.pi / reach)
    c, s = np.cos(grid), np.sin(grid)
    forward = np.block([[c, -s], [s, c]])
    inverse = np.block([[c, s], [-s, c]]) / LINES
    mats = []
    for m in (forward, inverse):
        high = m.astype(jnp.bfloat16)
        low = (m - high.astype(np.float64)).astype(jnp.bfloat16)
        mats.append(np.stack([high, low]))
    mats = np.stack(mats)
    base = np.outer(np.arange(n), np.arange(reach)) * (2.0 * np.pi / LINES)
    twiddle = np.stack([np.cos(base), np.sin(base)]).astype(np.float32)
    vmem = pl.BlockSpec(memory_space=pltpu.VMEM)
    out = pl.pallas_call(
        functools.partial(filter_kernel, n, dates, reach),
        out_shape=jax.ShapeDtypeStruct((2 * dates * RG, LINES), F32),
        in_specs=[pl.BlockSpec(memory_space=pltpu.SMEM)] + [vmem] * 5,
        out_specs=pl.BlockSpec(memory_space=pl.ANY),
        scratch_shapes=[
            pltpu.VMEM((2, n, dates, reach), F32),
            pltpu.VMEM((2, n, dates, reach), F32),
            pltpu.VMEM((2, n, dates, WIN), F32),
            pltpu.VMEM((n * dates, 2 * reach), BF16),
            pltpu.VMEM((n * dates, 2 * reach), BF16),
            pltpu.VMEM((n * dates, 2 * reach), F32),
            pltpu.VMEM((LINES // WIN, 2 * dates * RG, WIN), F32),
            pltpu.SemaphoreType.DMA((LINES // WIN,)),
        ],
        compiler_params=pltpu.CompilerParams(vmem_limit_bytes=40 * 1024 * 1024),
        name="shift_filter",
    )(starts, x, delay[:, None], angles, jnp.asarray(mats), jnp.asarray(twiddle))
    return out.reshape(2, dates, RG, LINES)


def solution(mesh):
    n = mesh.shape["date"]

    def on_device(g, z, wt, disp, delay, angles, starts):
        x = windows_call(n, g, z, wt, disp)
        return filter_call(n, x, delay, angles, starts)

    both = ("frames", "date")
    return jax.shard_map(
        on_device,
        mesh=mesh,
        in_specs=(
            P(both, None, None, None),
            P(both, None, None, None),
            P(both, None),
            P(both, None),
            P(both),
            P(both, None),
            P("frames"),
        ),
        out_specs=P(None, both, None, None),
        check_vma=False,
    )
```

time: 369 us -> 81.7 us (0.22)
  matrix products: 102 us -> 0 us
  local copies, waits for them, and re-layouts: 107 us -> 5.92 us
  waiting for transfers between devices: 88.9 us -> 0 us
  Pallas kernels: 0 us -> 75.5 us
  other arithmetic: 57.9 us -> 0 us
  starting transfers between devices: 13.7 us -> 0 us
    dot_general x19 -> x0, matrix products: 102 us -> none  [the longest x4 22.9 us: complex_product(): jnp.einsum(formula, left_imag, right_real, precision=UPPER_LIMIT)]
    all_to_all x1 -> x0, waiting for transfers between devices: 87.6 us -> none  [on_device(): lax.all_to_all(pixels, 'date', split_axis=1, concat_axis=3, tiled=True)]
    pallas_call x0 -> x2, Pallas kernels: none -> 75.5 us  [the longest x1 60.2 us: windows_call(): pl.pallas_call(functools.partial(windows_kernel, n, dates, wpd), out_shap...]
    mul x4 -> x0, local copies, waits for them, and re-layouts: 23.7 us -> none  [the longest x1 17.9 us: window_adjoint(): (blocks[:, :date_count, :date_count] + blocks[:, date_count:, date_count:...]
    mul x4 -> x0, other arithmetic: 20.1 us -> none  [the longest x1 13.2 us: window_adjoint(): adjusted_imag = cot_imag * scaling]
    convert_element_type x5 -> x0, other arithmetic: 15.5 us -> none  [the longest x1 5.47 us: window_adjoint(): cot_real = backward_sensitivity[:, 0].astype(jnp.float32)]
    slice x5 -> x0, local copies, waits for them, and re-layouts: 13 us -> none  [the longest x1 4.56 us: on_device(): pieces[:, :, :, block_index, :]]
    add x3 -> x0, other arithmetic: 12.4 us -> none  [the longest x1 5.37 us: window_adjoint(): cot_real + swap_real]
  transfers between devices with their start and end apart: 3 -> 0, of which waited for: 2 -> 0; matrix products, arithmetic and copies ran while one was open for 1% -> 0% of each run, Pallas kernels for 0% -> 0%
where the time goes in v1:
time: 81.7 us; the launch traced here: 81.4 us
  Pallas kernels  75.5 us (92%)
  local copies, waits for them, and re-layouts  5.92 us (7%)
    pallas_call x1, Pallas kernels, windows_call(): pl.pallas_call(functools.partial(windows_kernel, n, dates, wpd), out_shap...  60.2 us
    pallas_call x1, Pallas kernels, filter_call(): pl.pallas_call(functools.partial(filter_kernel, n, dates, reach), out_sha...  15.3 us
    unnamed x16, local copies, waits for them, and re-layouts  5.19 us

profile of v1, /device:TPU:15, one launch (start us, length us, event | category | flops | bytes accessed | tf_op | source)
XLA Modules:
  0.0 81.4 jit_solution(309924270033229462)
XLA Ops:
  0.0 0.7 copy.10.delay_ref
  0.7 0.0 copy-start
  0.7 2.2 %copy-done = bf16[16,2,256,256]{3,2,1,0:T(8,128)(2,1)S(1)} copy-done((bf16[16,2,256,256]{3,2,1,0:T(8,128)(2,1)S(1)}, bf16[16,2,256,256]{3,2,1,0:T(8,128)(2,1)}, u32[]{:S(2)}) %copy-start) | copy-done | bytes 4194328
  2.9 0.0 copy-start.1
  2.9 1.6 %copy-done.1 = bf16[16,2,256,128]{3,2,1,0:T(8,128)(2,1)S(1)} copy-done((bf16[16,2,256,128]{3,2,1,0:T(8,128)(2,1)S(1)}, bf16[16,2,256,128]{3,2,1,0:T(8,128)(2,1)}, u32[]{:S(2)}) %copy-start.1) | copy-done | bytes 2097176
  4.5 0.0 copy-start.4
  4.5 0.7 copy-done.4
  5.2 0.0 copy-start.5
  5.2 0.7 copy-done.5
  5.9 0.0 copy-start.2
  5.9 0.0 copy-start.3
  5.9 0.0 copy-start.6
  5.9 0.0 copy-start.7
  5.9 60.2 %windows.1.x_ref = bf16[2,16,8,32,128]{4,3,2,1,0:T(8,128)(2,1)S(1)} custom-call(bf16[16,2,256,256]{3,2,1,0:T(8,128)(2,1)S(1)} %copy-done, bf16[16,2,256,128]{3,2,1,0:T(8,128)(2,1)S(1)} %copy-done.1, f32[16,128]{1,0:T(8,128)S(1)} %copy-done.4, s32[16,128]{1,0:T(8,128)S(1)} %copy-done.5), custom_call_target="tpu_custom_call" | custom-call | tf_op jit(solution)/shard_map/windows/pallas_call | solution.py:171
  66.1 0.0 copy-done.2
  66.1 0.0 copy-done.3
  66.1 0.0 copy-done.6
  66.1 0.0 copy-done.7
  66.1 15.3 %shift_filter.1 = f32[256,4096]{1,0:T(8,128)} custom-call(s32[8]{0:T(128)S(1)} %copy-done.7, bf16[2,16,8,32,128]{4,3,2,1,0:T(8,128)(2,1)S(1)} %windows.1.x_ref, s32[16,1]{1,0:T(8,128)S(1)} %copy.10.delay_ref, f32[16,9]{1,0:T(8,128)S(1)} %copy-done.6, bf16[2,2,512,512]{3,2,1,0:T(8,128)(2,1)S(1)} %copy-done.2, f32[2,16,256]{2,1,0:T(8,128)S(1)} %copy-done.3), custom_call_target="tpu_custom_call" | custom-call | tf_op jit(solution)/shard_map/shift_filter/pallas_call | solution.py:341
Async XLA Ops:
  0.7 2.2 %copy-start = (bf16[16,2,256,256]{3,2,1,0:T(8,128)(2,1)S(1)}, bf16[16,2,256,256]{3,2,1,0:T(8,128)(2,1)}, u32[]{:S(2)}) copy-start(bf16[16,2,256,256]{3,2,1,0:T(8,128)(2,1)} %g_hbm.1) | copy-start | bytes 12582916
  2.9 1.6 %copy-start.1 = (bf16[16,2,256,128]{3,2,1,0:T(8,128)(2,1)S(1)}, bf16[16,2,256,128]{3,2,1,0:T(8,128)(2,1)}, u32[]{:S(2)}) copy-start(bf16[16,2,256,128]{3,2,1,0:T(8,128)(2,1)} %z_hbm.1) | copy-start | bytes 6291460
  4.5 0.7 copy-start.4
  5.2 0.7 copy-start.5
  5.9 60.2 %copy-start.2 = (bf16[2,2,512,512]{3,2,1,0:T(8,128)(2,1)S(1)}, bf16[2,2,512,512]{3,2,1,0:T(8,128)(2,1)}, u32[]{:S(2)}) copy-start(bf16[2,2,512,512]{3,2,1,0:T(8,128)(2,1)} %constant.4.clone.mats_ref) | copy-start | bytes 6291460
  5.9 60.2 %copy-start.3 = (f32[2,16,256]{2,1,0:T(8,128)S(1)}, f32[2,16,256]{2,1,0:T(8,128)}, u32[]{:S(2)}) copy-start(f32[2,16,256]{2,1,0:T(8,128)} %constant.5.clone.tw_ref) | copy-start | bytes 98308
  5.9 60.2 %copy-start.6 = (f32[16,9]{1,0:T(8,128)S(1)}, f32[16,9]{1,0:T(8,128)}, u32[]{:S(2)}) copy-start(f32[16,9]{1,0:T(8,128)} %angle_ref.1) | copy-start | bytes 1732
  5.9 60.2 %copy-start.7 = (s32[8]{0:T(128)S(1)}, s32[8]{0:T(128)}, u32[]{:S(2)}) copy-start(s32[8]{0:T(128)} %starts_ref.1) | copy-start | bytes 100

commit v2 on v1

--- a/solution.py
+++ b/solution.py
@@ -14,16 +14,47 @@
 WIN = 128
 QUANT = 16
 SEGMENTS = 9
+PIECE = 2
 MESH = pl.DeviceIdType.MESH
 F32 = jnp.float32
 BF16 = jnp.bfloat16
 
 
-def windows_kernel(
+def butterfly(real, imag, sign):
+    n = len(real)
+    if n == 1:
+        return real, imag
+    er, ei = butterfly(real[0::2], imag[0::2], sign)
+    our, oui = butterfly(real[1::2], imag[1::2], sign)
+    half = n // 2
+    out_r, out_i = [None] * n, [None] * n
+    for k in range(half):
+        xr, xi = our[k], oui[k]
+        if k == 0:
+            tr, ti = xr, xi
+        elif 4 * k == n:
+            tr, ti = (xi, -xr) if sign < 0 else (-xi, xr)
+        else:
+            angle = sign * 2.0 * np.pi * k / n
+            c, s = float(np.cos(angle)), float(np.sin(angle))
+            tr, ti = xr * c - xi * s, xr * s + xi * c
+        out_r[k], out_i[k] = er[k] + tr, ei[k] + ti
+        out_r[k + half], out_i[k + half] = er[k] - tr, ei[k] - ti
+    return out_r, out_i
+
+
+def split(value):
+    high = value.astype(BF16)
+    return high, (value - high.astype(F32)).astype(BF16)
+
+
+def kernel(
     n, dates, wpd,
-    g_hbm, z_hbm, wt_ref, disp_ref, x_hbm,
-    gbuf, zbuf, lo_last, hi, pix, halo_out, halo_in, sendbuf,
-    in_sem, halo_sem, send_sem, recv_sem, local_sem,
+    starts_ref, delay_ref, g_hbm, z_hbm, wt_hbm, disp_hbm, angle_hbm, out,
+    gbuf, zbuf, wt_ref, disp_ref, angle_ref, mats_ref, tw_ref,
+    lo_last, hi, pix, halo_out, halo_in, sendbuf, x_ref,
+    phase, twist, rotor, yh, yl, xp, u,
+    in_sem, table_sem, halo_sem, send_sem, recv_sem,
 ):
     me = lax.axis_index("date")
     chunks = wpd // 8
@@ -34,9 +65,19 @@
             pltpu.make_async_copy(z_hbm.at[w], zbuf.at[w], in_sem.at[w, 1]),
         )
 
+    table_copies = [
+        pltpu.make_async_copy(source, target, table_sem.at[i])
+        for i, (source, target) in enumerate((
+            (wt_hbm, wt_ref), (disp_hbm, disp_ref), (angle_hbm, angle_ref),
+        ))
+    ]
+    for copy in table_copies[:2]:
+        copy.start()
     for w in [wpd - 1] + list(range(wpd - 1)):
         for copy in input_copies(w):
             copy.start()
+    for copy in table_copies[2:]:
+        copy.start()
 
     barrier = pltpu.get_barrier_semaphore()
     for k in range(1, n):
@@ -89,6 +130,8 @@
             lax.dot_general(s1, chooser, dims, preferred_element_type=F32),
         )
 
+    for copy in table_copies[:2]:
+        copy.wait()
     spread = window(wpd - 1)
     for c in range(2):
         lo_last[pl.ds(c * EPOCHS, EPOCHS), :] = spread[c][:, :WIN]
@@ -102,11 +145,25 @@
 
     lane = lax.broadcasted_iota(jnp.int32, (2 * dates, WIN), 1)
 
-    def send_copy(g, k):
+    pieces = RG // PIECE
+
+    def partner(j):
+        return n // 2 + (2 * (j % 2) - 1) * (j // 2)
+
+    def chunk_copy(g, k):
         e = lax.rem(me + k, n)
         return pltpu.make_async_remote_copy(
-            src_ref=sendbuf.at[g, e], dst_ref=x_hbm.at[g, me],
+            src_ref=sendbuf.at[g, e], dst_ref=x_ref.at[g, me],
             send_sem=send_sem.at[g, k], recv_sem=recv_sem.at[g, k],
+            device_id={"date": e}, device_id_type=MESH,
+        )
+
+    def piece_copy(p, k):
+        e = lax.rem(me + k, n)
+        columns = pl.ds(p * PIECE, PIECE)
+        return pltpu.make_async_remote_copy(
+            src_ref=sendbuf.at[chunks - 1, e, columns], dst_ref=x_ref.at[chunks - 1, me, columns],
+            send_sem=send_sem.at[chunks - 1 + p, k], recv_sem=recv_sem.at[chunks - 1 + p, k],
             device_id={"date": e}, device_id_type=MESH,
         )
 
@@ -128,7 +185,7 @@
         if g == chunks - 1:
             pix[7] = lo_last[...] + hi[...]
 
-        def relayout(e):
+        def relayout(e, target):
             items = []
             for b in range(8):
                 items.append(jnp.concatenate([
@@ -143,96 +200,51 @@
                         items[b] = jnp.where(keep, low, pltpu.roll(high, 16 * bit, 1))
                         items[b + bit] = jnp.where(keep, pltpu.roll(low, WIN - 16 * bit, 1), high)
             for column in range(8):
-                sendbuf[g, e, column] = items[column].astype(BF16)
-
-        def send(k, carry):
-            relayout(lax.rem(me + k, n))
-            send_copy(g, k).start()
+                target[g, e, column] = items[column].astype(BF16)
+
+        def send(j, carry):
+            k = partner(j)
+            relayout(lax.rem(me + k, n), sendbuf)
+            if g < chunks - 1:
+                chunk_copy(g, k).start()
+            else:
+                piece_copy(0, k).start()
             return carry
 
         lax.fori_loop(1, n, send, 0)
-        relayout(me)
-        pltpu.make_async_copy(sendbuf.at[g, me], x_hbm.at[g, me], local_sem.at[g]).start()
-
-    for g in range(chunks):
-        pltpu.make_async_copy(sendbuf.at[g, me], x_hbm.at[g, me], local_sem.at[g]).wait()
-
-        def drain(k, carry):
-            send_copy(g, k).wait()
-            return carry
-
-        lax.fori_loop(1, n, drain, 0)
-
-
-def windows_call(n, g, z, wt, disp):
-    wpd = g.shape[0]
-    dates = EPOCHS // n
-    chunks = wpd // 8
-    return pl.pallas_call(
-        functools.partial(windows_kernel, n, dates, wpd),
-        out_shape=jax.ShapeDtypeStruct((chunks, n, RG, 2 * dates, WIN), BF16),
-        in_specs=[pl.BlockSpec(memory_space=pl.ANY)] * 2
-        + [pl.BlockSpec(memory_space=pltpu.VMEM)] * 2,
-        out_specs=pl.BlockSpec(memory_space=pl.ANY),
-        scratch_shapes=[
-            pltpu.VMEM((wpd, 2, EPOCHS, EPOCHS), BF16),
-            pltpu.VMEM((wpd, 2, EPOCHS, WIN), BF16),
-            pltpu.VMEM((2 * EPOCHS, WIN), F32),
-            pltpu.VMEM((2 * EPOCHS, WIN), F32),
-            pltpu.VMEM((8, 2 * EPOCHS, WIN), F32),
-            pltpu.VMEM((2 * EPOCHS, WIN), BF16),
-            pltpu.VMEM((2 * EPOCHS, WIN), BF16),
-            pltpu.VMEM((chunks, n, RG, 2 * dates, WIN), BF16),
-            pltpu.SemaphoreType.DMA((wpd, 2)),
-            pltpu.SemaphoreType.DMA((2,)),
-            pltpu.SemaphoreType.DMA((chunks, n)),
-            pltpu.SemaphoreType.DMA((chunks, n)),
-            pltpu.SemaphoreType.DMA((chunks,)),
-        ],
-        compiler_params=pltpu.CompilerParams(
-            collective_id=0, has_side_effects=True, vmem_limit_bytes=40 * 1024 * 1024
-        ),
-        name="windows",
-    )(g, z, wt, disp)
-
-
-def butterfly(real, imag, sign):
-    n = len(real)
-    if n == 1:
-        return real, imag
-    er, ei = butterfly(real[0::2], imag[0::2], sign)
-    our, oui = butterfly(real[1::2], imag[1::2], sign)
-    half = n // 2
-    out_r, out_i = [None] * n, [None] * n
-    for k in range(half):
-        xr, xi = our[k], oui[k]
-        if k == 0:
-            tr, ti = xr, xi
-        elif 4 * k == n:
-            tr, ti = (xi, -xr) if sign < 0 else (-xi, xr)
-        else:
-            angle = sign * 2.0 * np.pi * k / n
-            c, s = float(np.cos(angle)), float(np.sin(angle))
-            tr, ti = xr * c - xi * s, xr * s + xi * c
-        out_r[k], out_i[k] = er[k] + tr, ei[k] + ti
-        out_r[k + half], out_i[k + half] = er[k] - tr, ei[k] - ti
-    return out_r, out_i
-
-
-def split(value):
-    high = value.astype(BF16)
-    return high, (value - high.astype(F32)).astype(BF16)
-
-
-def filter_kernel(
-    n, dates, reach,
-    starts_ref, x_ref, delay_ref, angle_ref, mats_ref, tw_ref, o_hbm,
-    phase, twist, xp, yh, yl, u, out, out_sem,
-):
-    chunks = reach // WIN
+        relayout(me, x_ref)
+
+    def send_pieces(i, carry):
+        piece_copy(1 + i // (n - 1), partner(1 + i % (n - 1))).start()
+        return carry
+
+    lax.fori_loop(0, (pieces - 1) * (n - 1), send_pieces, 0)
+    for copy in table_copies[2:]:
+        copy.wait()
+    reach = LINES // n
     unit = float(2.0 * np.pi / (LINES * QUANT))
     period = LINES * QUANT
-    delay = delay_ref[...] + 8 * QUANT
+    index = lax.broadcasted_iota(jnp.int32, (dates, 1), 0)
+    delay = jnp.full((dates, 1), 8 * QUANT, jnp.int32)
+    for d in range(dates):
+        delay = delay + jnp.where(index == d, delay_ref[d], 0)
+    grid = lax.broadcasted_iota(jnp.int32, (reach, reach), 0) * lax.broadcasted_iota(
+        jnp.int32, (reach, reach), 1
+    )
+    grid = (grid & (reach - 1)).astype(F32) * float(2.0 * np.pi / reach)
+    grid_c, grid_s = jnp.cos(grid), jnp.sin(grid)
+    for which, (a, b, c, d) in enumerate((
+        (grid_c, -grid_s, grid_s, grid_c),
+        (grid_c * (1.0 / LINES), grid_s * (1.0 / LINES), grid_s * (-1.0 / LINES), grid_c * (1.0 / LINES)),
+    )):
+        for i, block in enumerate((a, b, c, d)):
+            rows, lanes = pl.ds(i // 2 * reach, reach), pl.ds(i % 2 * reach, reach)
+            mats_ref[which, 0, rows, lanes], mats_ref[which, 1, rows, lanes] = split(block)
+    base = lax.broadcasted_iota(jnp.int32, (n, reach), 0) * lax.broadcasted_iota(
+        jnp.int32, (n, reach), 1
+    )
+    base = base.astype(F32) * float(2.0 * np.pi / LINES)
+    tw_ref[0], tw_ref[1] = jnp.cos(base), jnp.sin(base)
     cosines, sines = jnp.cos(angle_ref[...]), jnp.sin(angle_ref[...])
     for s in range(n):
         position = s * reach + lax.broadcasted_iota(jnp.int32, (dates, reach), 1) - 8
@@ -255,8 +267,8 @@
     lanes = lax.broadcasted_iota(jnp.int32, (dates, reach), 1)
     lanes = jnp.where(lanes < reach // 2, lanes, lanes - reach) * n
     lane_angle = ((lanes * delay) & (period - 1)).astype(F32) * unit
-    lane_c = jnp.concatenate([jnp.cos(lane_angle)] * n, axis=0)
-    lane_s = jnp.concatenate([jnp.sin(lane_angle)] * n, axis=0)
+    rotor[0] = jnp.concatenate([jnp.cos(lane_angle)] * n, axis=0)
+    rotor[1] = jnp.concatenate([jnp.sin(lane_angle)] * n, axis=0)
 
     def product(which):
         high, low = yh[...], yl[...]
@@ -289,6 +301,7 @@
                     )
         yh[...], yl[...] = split(u[...])
         spec = product(0)
+        lane_c, lane_s = rotor[0], rotor[1]
         sr, si = spec[:, :reach], spec[:, reach:]
         rh, rl = split(sr * lane_c - si * lane_s)
         ih, il = split(sr * lane_s + si * lane_c)
@@ -308,63 +321,85 @@
                 vr, vi = butterfly(vr, vi, 1)
                 for h in range(n):
                     for c, v in ((0, vr[h]), (1, vi[h])):
-                        out[h * chunks + lt, pl.ds((c * dates + dh * 8) * RG + col, 8, stride=RG), :] = v
+                        tile = (c * dates + dh * 8) * (LINES // WIN) + h * chunks + lt
+                        out[pl.ds(tile * RG + col, 8, stride=RG * (LINES // WIN)), :] = v
         return carry
 
-    lax.fori_loop(0, RG, column, 0)
-    copies = [
-        pltpu.make_async_copy(out.at[t], o_hbm.at[:, pl.ds(t * WIN, WIN)], out_sem.at[t])
-        for t in range(LINES // WIN)
-    ]
-    for copy in copies:
-        copy.start()
-    for copy in copies:
-        copy.wait()
-
-
-def filter_call(n, x, delay, angles, starts):
-    dates = delay.shape[0]
+    for g in range(chunks - 1):
+
+        def drain(k, carry):
+            chunk_copy(g, k).wait()
+            return carry
+
+        lax.fori_loop(1, n, drain, 0)
+
+    def piece(p, carry):
+        def drain(k, carry):
+            piece_copy(p, k).wait()
+            return carry
+
+        lax.fori_loop(1, n, drain, 0)
+        lax.fori_loop(p * PIECE, (p + 1) * PIECE, column, 0)
+        return carry
+
+    lax.fori_loop(0, pieces, piece, 0)
+
+
+def call(n, g, z, wt, disp, delay, angles, starts):
+    wpd = g.shape[0]
+    chunks = wpd // 8
+    dates = EPOCHS // n
     reach = LINES // n
-    grid = np.outer(np.arange(reach), np.arange(reach)) % reach * (2.0 * np.pi / reach)
-    c, s = np.cos(grid), np.sin(grid)
-    forward = np.block([[c, -s], [s, c]])
-    inverse = np.block([[c, s], [-s, c]]) / LINES
-    mats = []
-    for m in (forward, inverse):
-        high = m.astype(jnp.bfloat16)
-        low = (m - high.astype(np.float64)).astype(jnp.bfloat16)
-        mats.append(np.stack([high, low]))
-    mats = np.stack(mats)
-    base = np.outer(np.arange(n), np.arange(reach)) * (2.0 * np.pi / LINES)
-    twiddle = np.stack([np.cos(base), np.sin(base)]).astype(np.float32)
-    vmem = pl.BlockSpec(memory_space=pltpu.VMEM)
+    smem = pl.BlockSpec(memory_space=pltpu.SMEM)
+    hbm = pl.BlockSpec(memory_space=pl.ANY)
+    messages = chunks - 1 + RG // PIECE
     out = pl.pallas_call(
-        functools.partial(filter_kernel, n, dates, reach),
-        out_shape=jax.ShapeDtypeStruct((2 * dates * RG, LINES), F32),
-        in_specs=[pl.BlockSpec(memory_space=pltpu.SMEM)] + [vmem] * 5,
-        out_specs=pl.BlockSpec(memory_space=pl.ANY),
+        functools.partial(kernel, n, dates, wpd),
+        out_shape=jax.ShapeDtypeStruct((2 * dates * RG * (LINES // WIN), WIN), F32),
+        in_specs=[smem] * 2 + [hbm] * 5,
+        out_specs=pl.BlockSpec(memory_space=pltpu.VMEM),
         scratch_shapes=[
+            pltpu.VMEM((wpd, 2, EPOCHS, EPOCHS), BF16),
+            pltpu.VMEM((wpd, 2, EPOCHS, WIN), BF16),
+            pltpu.VMEM((wpd, WIN), F32),
+            pltpu.VMEM((wpd, WIN), jnp.int32),
+            pltpu.VMEM((dates, SEGMENTS), F32),
+            pltpu.VMEM((2, 2, 2 * reach, 2 * reach), BF16),
+            pltpu.VMEM((2, n, reach), F32),
+            pltpu.VMEM((2 * EPOCHS, WIN), F32),
+            pltpu.VMEM((2 * EPOCHS, WIN), F32),
+            pltpu.VMEM((8, 2 * EPOCHS, WIN), F32),
+            pltpu.VMEM((2 * EPOCHS, WIN), BF16),
+            pltpu.VMEM((2 * EPOCHS, WIN), BF16),
+            pltpu.VMEM((chunks, n, RG, 2 * dates, WIN), BF16),
+            pltpu.VMEM((chunks, n, RG, 2 * dates, WIN), BF16),
             pltpu.VMEM((2, n, dates, reach), F32),
             pltpu.VMEM((2, n, dates, reach), F32),
-            pltpu.VMEM((2, n, dates, WIN), F32),
+            pltpu.VMEM((2, n * dates, reach), F32),
             pltpu.VMEM((n * dates, 2 * reach), BF16),
             pltpu.VMEM((n * dates, 2 * reach), BF16),
+            pltpu.VMEM((2, n, dates, WIN), F32),
             pltpu.VMEM((n * dates, 2 * reach), F32),
-            pltpu.VMEM((LINES // WIN, 2 * dates * RG, WIN), F32),
-            pltpu.SemaphoreType.DMA((LINES // WIN,)),
+            pltpu.SemaphoreType.DMA((wpd, 2)),
+            pltpu.SemaphoreType.DMA((3,)),
+            pltpu.SemaphoreType.DMA((2,)),
+            pltpu.SemaphoreType.DMA((messages, n)),
+            pltpu.SemaphoreType.DMA((messages, n)),
         ],
-        compiler_params=pltpu.CompilerParams(vmem_limit_bytes=40 * 1024 * 1024),
-        name="shift_filter",
-    )(starts, x, delay[:, None], angles, jnp.asarray(mats), jnp.asarray(twiddle))
-    return out.reshape(2, dates, RG, LINES)
+        compiler_params=pltpu.CompilerParams(
+            collective_id=0, has_side_effects=True, vmem_limit_bytes=60 * 1024 * 1024
+        ),
+        name="adjoint",
+    )(starts, delay, g, z, wt, disp, angles)
+    out = out.reshape(2, dates, LINES // WIN, RG, WIN)
+    return jnp.transpose(out, (0, 1, 3, 2, 4)).reshape(2, dates, RG, LINES)
 
 
 def solution(mesh):
     n = mesh.shape["date"]
 
     def on_device(g, z, wt, disp, delay, angles, starts):
-        x = windows_call(n, g, z, wt, disp)
-        return filter_call(n, x, delay, angles, starts)
+        return call(n, g, z, wt, disp, delay, angles, starts)
 
     both = ("frames", "date")
     return jax.shard_map(

time: 81.7 us -> 74 us (0.906)
  the two profiles are of different devices: /device:TPU:15 before, /device:TPU:0 now
where the time goes in v2:
time: 74 us; the launch traced here: 73.8 us
  Pallas kernels  69.1 us (93%)
  local copies, waits for them, and re-layouts  4.65 us (6%)
    pallas_call x1, Pallas kernels, call(): pl.pallas_call(functools.partial(kernel, n, dates, wpd), out_shape=jax.Sh...  69.1 us
    unnamed x1, local copies, waits for them, and re-layouts  4.65 us

profile of v2, /device:TPU:0, one launch (start us, length us, event | category | flops | bytes accessed | tf_op | source)
XLA Modules:
  0.0 73.8 jit_solution(8748534480878634539)
XLA Ops:
  0.0 69.1 %adjoint.1 = f32[8192,128]{1,0:T(8,128)} custom-call(s32[8]{0:T(128)} %starts_ref.1, s32[16]{0:T(128)} %delay_ref.1, bf16[16,2,256,256]{3,2,1,0:T(8,128)(2,1)} %g_hbm.1, bf16[16,2,256,128]{3,2,1,0:T(8,128)(2,1)} %z_hbm.1, f32[16,128]{1,0:T(8,128)} %wt_hbm.1, s32[16,128]{1,0:T(8,128)} %disp_hbm.1, f32[16,9]{1,0:T(8,128)} %angle_hbm.1), custom_call_target="tpu_custom_call" | custom-call | tf_op jit(solution)/shard_map/adjoint/pallas_call | solution.py:356
  69.1 4.7 %copy.9 = f32[2,16,8,4096]{3,2,1,0:T(8,128)} copy(f32[2,16,8,4096]{3,2,1,0:T(8,128)} %bitcast.5) | data formatting | bytes 8388608
